TPU v7x, 32 devices: a whole 2x2x4 slice. The times are simulated.
32 devices in a mesh: seq: 8 (over z, x), head: 4 (over y, core).
Axes of the slice: x: 2, y: 2, z: 4, core: 2. Of those that a mesh axis runs over, the one named last changes fastest.
Arguments:
- queries: bfloat16 [2048, 128], P('seq'), may hold values from -4 to 4
- keys: bfloat16 [2048, 128], P('seq'), may hold values from -4 to 4
- values: bfloat16 [2048, 2048], P('seq', 'head'), may hold values from -0.75 to 0.75
- level_codes: int32 [32, 12, 2048], P('head', None, 'seq'), may hold values from 1 to 15
- cotangent: bfloat16 [2048, 2048], P('seq', 'head'), may hold values from -0.75 to 0.75
Outputs:
- attended: bfloat16 [2048, 2048], P('seq', 'head')
- query_grad: float32 [2048, 128], P(('seq', 'head'))
- key_grad: float32 [2048, 128], P(('seq', 'head'))
- value_grad: bfloat16 [2048, 2048], P('seq', 'head')
All inputs are finite; a program needn't handle non-finite values.
Results may differ from a plain program's by a relative error of at most 0.0057.
Values sent between devices are 32-bit elements; how exact they have to be, the bound alone decides.
A program may use at most 64 MiB of HBM per device.

v0:
```python
import functools

import jax
import jax.numpy as jnp
from jax import lax
from jax.experimental import pallas as pl
from jax.experimental.pallas import tpu as pltpu
from jax.sharding import PartitionSpec as P

STRETCH_BITS = 7
STRETCH = 128
LANES = 128
SCALE_CODE = 0.125
MESH = pl.DeviceIdType.MESH


def dot(a, b, da, db):
    return lax.dot_general(a, b, (((da,), (db,)), ((), ())), preferred_element_type=jnp.float32)


def kernel(
    n_seq, n_head,
    q_in, k_in, v_in, code_in, g_in,
    att_out, qg_out, kg_out, vg_out,
    att, vg, qg, kg, wts, lams, own, got, pend, back, racc, qk_send, qk_recv,
    f_send, f_recv, b_send, b_recv, h_send, h_recv,
    q_ref, k_ref, v_ref, code_ref, g_ref, load,
):
    loads = [
        pltpu.make_async_copy(src, dst, load.at[i])
        for i, (src, dst) in enumerate((
            (k_in, k_ref), (v_in, v_ref), (g_in, g_ref), (q_in, q_ref), (code_in, code_ref)))
    ]
    for one in loads:
        one.start()
    tokens, depth = q_ref.shape
    total_width = v_ref.shape[1]
    heads = code_ref.shape[1]
    width = total_width // heads
    chunks = total_width // LANES
    per_chunk = LANES // width
    blocks = tokens // STRETCH
    rows = tokens // n_head
    bits = n_seq.bit_length() - 1
    scale = depth ** -0.5
    near = STRETCH_BITS + 1
    far = near + 1
    f32, bf16 = jnp.float32, jnp.bfloat16
    seq, head = lax.axis_index("seq"), lax.axis_index("head")
    bit = [lax.rem(lax.div(seq, 1 << b), 2) for b in range(bits)]
    low_bits = bits - 2
    top, mid = bits - 1, bits - 2
    stride = 1 << mid
    line = lax.div(seq, stride)
    partner = [seq + (1 << b) * (1 - 2 * bit[b]) for b in range(low_bits)]
    peers = [lax.rem(head + j, n_head) for j in range(1, n_head)]

    barrier = pltpu.get_barrier_semaphore()

    def greet(to):
        pl.semaphore_signal(barrier, inc=1, device_id=to, device_id_type=MESH)

    for b in range(low_bits):
        greet((partner[b], head))
    for peer in peers:
        greet((seq, peer))

    @pl.when(line > 0)
    def _():
        greet((seq - stride, head))

    @pl.when(line < 3)
    def _():
        greet((seq + stride, head))

    greetings = low_bits + n_head - 1 + (line > 0).astype(jnp.int32) + (line < 3).astype(jnp.int32)

    def forward(b, c, relay=False):
        return pltpu.make_async_remote_copy(
            src_ref=(got if relay else own).at[b, c], dst_ref=got.at[b, c],
            send_sem=f_send.at[b, c], recv_sem=f_recv.at[b, c],
            device_id=(partner[b] if b < low_bits else seq + stride, head), device_id_type=MESH)

    def backward(b, c):
        return pltpu.make_async_remote_copy(
            src_ref=pend.at[b, c], dst_ref=back.at[b, c],
            send_sem=b_send.at[b, c], recv_sem=b_recv.at[b, c],
            device_id=(partner[b] if b < low_bits else seq - stride, head), device_id_type=MESH)

    highest = [lax.div(seq, 2 << b) == (n_seq >> (b + 1)) - 1 for b in range(low_bits)]
    up_sends = [jnp.logical_or(bit[b] == 0, jnp.logical_not(highest[b])) for b in range(low_bits)]
    up_gets = [jnp.logical_or(bit[b] == 1, jnp.logical_not(highest[b])) for b in range(low_bits)]
    down_sends, down_gets = up_gets, up_sends

    cols = [slice(c * LANES, (c + 1) * LANES) for c in range(chunks)]

    spread = (
        lax.broadcasted_iota(jnp.int32, (heads, total_width), 1) // width
        == lax.broadcasted_iota(jnp.int32, (heads, total_width), 0)
    ).astype(f32)

    def level_weights(level):
        lam = code_ref[level].astype(f32) * SCALE_CODE
        return dot(lam, spread, 0, 0)

    def prepare(b):
        @pl.when(bit[b] == 1)
        def _():
            lam = level_weights(far + b)
            lams[b] = lam.astype(bf16)
            weighted = (g_ref[...].astype(f32) * lam).astype(bf16)
            wts[b] = weighted
            sending = dot(q_ref[...], weighted, 0, 0) * scale
            for c in range(chunks):
                pend[b, c] = sending[:, cols[c]]

        if b < low_bits:
            @pl.when(bit[b] == 0)
            def _():
                for c in range(chunks):
                    pend[b, c] = jnp.zeros((depth, LANES), f32)

    first_half = slice(0, STRETCH)
    second_half = slice(STRETCH, 2 * STRETCH)
    loads[0].wait()
    loads[1].wait()
    state_low = dot(k_ref[first_half, :], v_ref[first_half, :], 0, 0)
    state_all = state_low + dot(k_ref[second_half, :], v_ref[second_half, :], 0, 0)
    for c in range(chunks):
        own[0, c] = state_all[:, cols[c]]
    pl.semaphore_wait(barrier, greetings)
    for c in range(chunks):
        @pl.when(up_sends[0])
        def _(c=c):
            forward(0, c).start()
    for one in loads[2:]:
        one.wait()
    prepare(top)
    for c in range(chunks):
        @pl.when(line == 3)
        def _(c=c):
            backward(top, c).start()
    prepare(mid)
    for c in range(chunks):
        @pl.when(line == 3)
        def _(c=c):
            backward(mid, c).start()
    for b in range(low_bits - 1, -1, -1):
        prepare(b)

    key_pos = lax.rem(lax.broadcasted_iota(jnp.int32, (per_chunk * STRETCH, STRETCH), 0), STRETCH)
    query_pos = lax.broadcasted_iota(jnp.int32, (per_chunk * STRETCH, STRETCH), 1)
    differ = jnp.bitwise_xor(query_pos, key_pos)
    causal = key_pos <= query_pos
    lane_head = lax.broadcasted_iota(jnp.int32, (STRETCH, LANES), 1) // width

    def split_heads(block):
        block = block.astype(f32)
        return jnp.concatenate(
            [jnp.where(lane_head == i, block, 0.0) for i in range(per_chunk)], axis=0).astype(bf16)

    press_sum = [jnp.zeros((STRETCH, STRETCH), f32) for _ in range(blocks)]
    scores = []
    for n in range(blocks):
        at = slice(n * STRETCH, (n + 1) * STRETCH)
        one = dot(k_ref[at, :], q_ref[at, :], 1, 1) * scale
        scores.append(jnp.concatenate([one] * per_chunk, axis=0))

    def unit(n, c):
        at = slice(n * STRETCH, (n + 1) * STRETCH)

        def rows_of(level):
            parts = []
            for i in range(per_chunk):
                row = code_ref[level, c * per_chunk + i:c * per_chunk + i + 1, at].astype(f32) * SCALE_CODE
                parts.append(jnp.broadcast_to(row, (STRETCH, STRETCH)))
            return jnp.concatenate(parts, axis=0)

        mask = rows_of(STRETCH_BITS)
        for level in range(STRETCH_BITS - 1, -1, -1):
            mask = jnp.where(differ < (1 << level), rows_of(level), mask)
        mask = jnp.where(causal, mask, 0.0)
        mixed = (scores[n] * mask).astype(bf16)
        v_split = split_heads(v_ref[at, cols[c]])
        g_block = g_ref[at, cols[c]]
        att[at, cols[c]] = dot(mixed, v_split, 0, 0)
        wide = jnp.concatenate(
            [mixed[i * STRETCH:(i + 1) * STRETCH] for i in range(per_chunk)], axis=1)
        vg[at, cols[c]] = dot(wide, split_heads(g_block), 1, 0)
        press = dot(v_split, g_block, 1, 1) * mask
        for i in range(per_chunk):
            press_sum[n] = press_sum[n] + press[i * STRETCH:(i + 1) * STRETCH]

    def finish_block(n):
        at = slice(n * STRETCH, (n + 1) * STRETCH)
        press = press_sum[n].astype(bf16)
        qg[at, :] = dot(press, k_ref[at, :], 0, 0) * scale
        kg[at, :] = dot(press, q_ref[at, :], 1, 0) * scale

    def near_level():
        low = state_low.astype(bf16)
        lam = level_weights(near)[second_half]
        att[second_half, :] = att[second_half, :] + lam * (
            dot(q_ref[second_half, :], low, 1, 0) * scale)
        weighted = (g_ref[second_half, :].astype(f32) * lam).astype(bf16)
        qg[second_half, :] = qg[second_half, :] + dot(weighted, low, 1, 1) * scale
        return dot(q_ref[second_half, :], weighted, 0, 0) * scale

    def consume(b):
        @pl.when(bit[b] == 1)
        def _():
            total = jnp.zeros((tokens, depth), f32)
            for c in range(chunks):
                state = got[b, c].astype(bf16)
                reading = dot(q_ref[...], state, 1, 0) * scale
                att[:, cols[c]] = att[:, cols[c]] + reading * lams[b, :, cols[c]].astype(f32)
                total = total + dot(wts[b, :, cols[c]], state, 1, 1)
            qg[...] = qg[...] + total * scale

    def share(which, j):
        return pltpu.make_async_remote_copy(
            src_ref=qk_send.at[which, peers[j]], dst_ref=qk_recv.at[which, j],
            send_sem=h_send.at[which, j], recv_sem=h_recv.at[which, j],
            device_id=(seq, peers[j]), device_id_type=MESH)

    def send_share(which, grad):
        for i in range(n_head):
            qk_send[which, i] = grad[i * rows:(i + 1) * rows]
        for j in range(n_head - 1):
            share(which, j).start()

    def step_forward(stage, c):
        if stage < low_bits:
            b = stage

            @pl.when(up_gets[b])
            def _():
                forward(b, c).wait_recv()
                own[b + 1, c] = own[b, c] + got[b, c]

            if b + 1 < low_bits:
                @pl.when(up_sends[b + 1])
                def _():
                    forward(b + 1, c).start()
            else:
                @pl.when(bit[mid] == 0)
                def _():
                    forward(mid, c).start()
        elif stage == low_bits:
            @pl.when(bit[mid] == 1)
            def _():
                forward(mid, c).wait_recv()

            @pl.when(line == 1)
            def _():
                own[top, c] = own[mid, c] + got[mid, c]
                forward(top, c).start()
        elif stage == low_bits + 1:
            @pl.when(line == 2)
            def _():
                forward(top, c).wait_recv()
                forward(top, c, True).start()
        else:
            @pl.when(line == 3)
            def _():
                forward(top, c).wait_recv()

    def pass_down(b, c):
        pend[b, c] = pend[b, c] + racc[c]

        @pl.when(down_sends[b])
        def _():
            backward(b, c).start()

    def step_backward(stage, c):
        if stage == 0:
            @pl.when(line == 2)
            def _():
                backward(top, c).wait_recv()
                pend[top, c] = pend[top, c] + back[top, c]
                backward(top, c).start()

            @pl.when(line == 3)
            def _():
                racc[c] = jnp.zeros((depth, LANES), f32)
                pass_down(low_bits - 1, c)
        elif stage == 1:
            @pl.when(line == 1)
            def _():
                backward(top, c).wait_recv()
                pend[mid, c] = pend[mid, c] + back[top, c]
                backward(mid, c).start()
                racc[c] = back[top, c]
                pass_down(low_bits - 1, c)

            @pl.when(line == 2)
            def _():
                backward(mid, c).wait_recv()
                racc[c] = back[mid, c]
                pass_down(low_bits - 1, c)
        elif stage == 2:
            @pl.when(line == 0)
            def _():
                backward(mid, c).wait_recv()
                racc[c] = back[mid, c]
                pass_down(low_bits - 1, c)
        else:
            b = low_bits - 1 - (stage - 3)

            @pl.when(down_gets[b])
            def _():
                backward(b, c).wait_recv()
                racc[c] = racc[c] + back[b, c]

            if b > 0:
                pass_down(b - 1, c)

    near_sum = None
    stages = low_bits + 3
    for c in range(chunks):
        unit(0, c)
    finish_block(0)
    for c in range(chunks):
        step_backward(0, c)
        step_forward(0, c)
    for stage in range(1, low_bits):
        for c in range(chunks):
            step_forward(stage, c)
    for c in range(chunks):
        step_backward(1, c)
        step_forward(low_bits, c)
    for c in range(chunks):
        step_backward(2, c)
        step_forward(low_bits + 1, c)
    for c in range(chunks):
        unit(1, c)
    finish_block(1)
    near_sum = near_level()
    for b in range(low_bits):
        consume(b)
    consume(mid)
    for c in range(chunks):
        step_forward(low_bits + 2, c)
    consume(top)
    send_share(0, qg[...])
    att_out[...] = att[...].astype(bf16)
    for stage in range(3, stages):
        for c in range(chunks):
            step_backward(stage, c)

    grad_low = kg[first_half, :]
    grad_high = kg[second_half, :]
    for c in range(chunks):
        incoming = racc[c]
        low = (incoming + near_sum[:, cols[c]]).astype(bf16)
        high = incoming.astype(bf16)
        grad_low = grad_low + dot(v_ref[first_half, cols[c]], low, 1, 1)
        grad_high = grad_high + dot(v_ref[second_half, cols[c]], high, 1, 1)
    send_share(1, jnp.concatenate([grad_low, grad_high], axis=0))
    for c in range(chunks):
        incoming = racc[c]
        low = (incoming + near_sum[:, cols[c]]).astype(bf16)
        high = incoming.astype(bf16)
        vg_out[first_half, cols[c]] = (
            vg[first_half, cols[c]] + dot(k_ref[first_half, :], low, 1, 0)).astype(bf16)
        vg_out[second_half, cols[c]] = (
            vg[second_half, cols[c]] + dot(k_ref[second_half, :], high, 1, 0)).astype(bf16)

    for which, out in ((0, qg_out), (1, kg_out)):
        total = qk_send[which, head]
        for j in range(n_head - 1):
            share(which, j).wait_recv()
            total = total + qk_recv[which, j]
        out[...] = total
    for which in range(2):
        for j in range(n_head - 1):
            share(which, j).wait_send()
    for c in range(chunks):
        for b in range(low_bits):
            @pl.when(up_sends[b])
            def _(b=b, c=c):
                forward(b, c).wait_send()

            @pl.when(down_sends[b])
            def _(b=b, c=c):
                backward(b, c).wait_send()

        @pl.when(bit[mid] == 0)
        def _(c=c):
            forward(mid, c).wait_send()

        @pl.when(bit[mid] == 1)
        def _(c=c):
            backward(mid, c).wait_send()

        @pl.when(line == 1)
        def _(c=c):
            forward(top, c).wait_send()

        @pl.when(line == 2)
        def _(c=c):
            forward(top, c, True).wait_send()

        @pl.when(line >= 2)
        def _(c=c):
            backward(top, c).wait_send()


def per_device(n_seq, n_head, queries, keys, values, level_codes, cotangent):
    tokens, depth = queries.shape
    total_width = values.shape[1]
    chunks = total_width // LANES
    rows = tokens // n_head
    bits = n_seq.bit_length() - 1
    f32, bf16 = jnp.float32, jnp.bfloat16
    vmem = pl.BlockSpec(memory_space=pltpu.VMEM)
    links = (bits, chunks, depth, LANES)
    dma = pltpu.SemaphoreType.DMA
    return pl.pallas_call(
        functools.partial(kernel, n_seq, n_head),
        out_shape=(
            jax.ShapeDtypeStruct((tokens, total_width), bf16),
            jax.ShapeDtypeStruct((rows, depth), f32),
            jax.ShapeDtypeStruct((rows, depth), f32),
            jax.ShapeDtypeStruct((tokens, total_width), bf16),
        ),
        in_specs=[pl.BlockSpec(memory_space=pltpu.HBM)] * 5,
        out_specs=(vmem,) * 4,
        scratch_shapes=[
            pltpu.VMEM((tokens, total_width), f32),
            pltpu.VMEM((tokens, total_width), f32),
            pltpu.VMEM((tokens, depth), f32),
            pltpu.VMEM((tokens, depth), f32),
            pltpu.VMEM((bits, tokens, total_width), bf16),
            pltpu.VMEM((bits, tokens, total_width), bf16),
            pltpu.VMEM(links, f32),
            pltpu.VMEM(links, f32),
            pltpu.VMEM(links, f32),
            pltpu.VMEM(links, f32),
            pltpu.VMEM((chunks, depth, LANES), f32),
            pltpu.VMEM((2, n_head, rows, depth), f32),
            pltpu.VMEM((2, n_head - 1, rows, depth), f32),
            dma((bits, chunks)),
            dma((bits, chunks)),
            dma((bits, chunks)),
            dma((bits, chunks)),
            dma((2, n_head - 1)),
            dma((2, n_head - 1)),
            pltpu.VMEM((tokens, depth), bf16),
            pltpu.VMEM((tokens, depth), bf16),
            pltpu.VMEM((tokens, total_width), bf16),
            pltpu.VMEM((level_codes.shape[1], level_codes.shape[0], tokens), jnp.int32),
            pltpu.VMEM((tokens, total_width), bf16),
            dma((5,)),
        ],
        compiler_params=pltpu.CompilerParams(
            collective_id=0, has_side_effects=True, vmem_limit_bytes=40 * 1024 * 1024),
    )(queries, keys, values, jnp.transpose(level_codes, (1, 0, 2)), cotangent)


def solution(mesh):
    placed = (
        P("seq", None),
        P("seq", None),
        P("seq", "head"),
        P("head", None, "seq"),
        P("seq", "head"),
    )
    return jax.shard_map(
        functools.partial(per_device, mesh.shape["seq"], mesh.shape["head"]),
        mesh=mesh,
        in_specs=placed,
        out_specs=(
            P("seq", "head"),
            P(("seq", "head"), None),
            P(("seq", "head"), None),
            P("seq", "head"),
        ),
        check_vma=False,
    )
```

profile of v0, /device:TPU:27, one launch (start us, length us, event | category | flops | bytes accessed | tf_op | source)
XLA Modules:
  0.0 34.8 jit_solution(9665805179308299587)
XLA Ops:
  0.6 0.0 copy-start
  0.6 0.9 %copy-done = bf16[256,512]{1,0:T(8,128)(2,1)S(1)} copy-done((bf16[256,512]{1,0:T(8,128)(2,1)S(1)}, bf16[256,512]{1,0:T(8,128)(2,1)}, u32[]{:S(2)}) %copy-start) | copy-done | bytes 262168
  1.6 0.0 copy-start.1
  1.6 0.9 %copy-done.1 = bf16[256,512]{1,0:T(8,128)(2,1)S(1)} copy-done((bf16[256,512]{1,0:T(8,128)(2,1)S(1)}, bf16[256,512]{1,0:T(8,128)(2,1)}, u32[]{:S(2)}) %copy-start.1) | copy-done | bytes 262168
  2.5 0.0 copy-start.2
  2.5 0.9 %copy-done.2 = s32[8,12,256]{2,0,1:T(8,128)S(1)} copy-done((s32[8,12,256]{2,0,1:T(8,128)S(1)}, s32[8,12,256]{2,0,1:T(8,128)}, u32[]{:S(2)}) %copy-start.2) | copy-done | bytes 98328
  3.4 0.0 copy-start.3
  3.4 0.8 %copy-done.3 = bf16[256,128]{1,0:T(8,128)(2,1)S(1)} copy-done((bf16[256,128]{1,0:T(8,128)(2,1)S(1)}, bf16[256,128]{1,0:T(8,128)(2,1)}, u32[]{:S(2)}) %copy-start.3) | copy-done | bytes 65560
  4.3 0.0 copy-start.4
  4.3 0.8 %copy-done.4 = bf16[256,128]{1,0:T(8,128)(2,1)S(1)} copy-done((bf16[256,128]{1,0:T(8,128)(2,1)S(1)}, bf16[256,128]{1,0:T(8,128)(2,1)}, u32[]{:S(2)}) %copy-start.4) | copy-done | bytes 65560
  5.1 27.0 %shard_map.84 = (bf16[256,512]{1,0:T(8,128)(2,1)S(1)}, f32[64,128]{1,0:T(8,128)S(1)}, f32[64,128]{1,0:T(8,128)S(1)}, bf16[256,512]{1,0:T(8,128)(2,1)S(1)}) custom-call(bf16[256,128]{1,0:T(8,128)(2,1)S(1)} %copy-done.3, bf16[256,128]{1,0:T(8,128)(2,1)S(1)} %copy-done.4, bf16[256,512]{1,0:T(8,128)(2,1)S(1)} %copy-done, s32[12,8,256]{2,1,0:T(8,128)S(1)} %bitcast.1, ...), custom_call_target="tpu_custom_call" | custom-call | tf_op jit(solution)/shard_map/pallas_call | solution.py:419
  32.1 0.7 %copy.13 = bf16[256,512]{1,0:T(8,128)(2,1)} copy(bf16[256,512]{1,0:T(8,128)(2,1)S(1)} %get-tuple-element.8) | data formatting | bytes 524288
  32.8 0.6 %copy.14 = f32[64,128]{1,0:T(8,128)} copy(f32[64,128]{1,0:T(8,128)S(1)} %get-tuple-element.9) | data formatting | bytes 65536
  33.5 0.6 %copy.15 = f32[64,128]{1,0:T(8,128)} copy(f32[64,128]{1,0:T(8,128)S(1)} %get-tuple-element.10) | data formatting | bytes 65536
  34.1 0.7 %copy.16 = bf16[256,512]{1,0:T(8,128)(2,1)} copy(bf16[256,512]{1,0:T(8,128)(2,1)S(1)} %get-tuple-element.11) | data formatting | bytes 524288
Async XLA Ops:
  0.6 1.0 %copy-start = (bf16[256,512]{1,0:T(8,128)(2,1)S(1)}, bf16[256,512]{1,0:T(8,128)(2,1)}, u32[]{:S(2)}) copy-start(bf16[256,512]{1,0:T(8,128)(2,1)} %v_in.1) | copy-start | bytes 786436
  1.6 0.9 %copy-start.1 = (bf16[256,512]{1,0:T(8,128)(2,1)S(1)}, bf16[256,512]{1,0:T(8,128)(2,1)}, u32[]{:S(2)}) copy-start(bf16[256,512]{1,0:T(8,128)(2,1)} %g_in.1) | copy-start | bytes 786436
  2.5 0.9 %copy-start.2 = (s32[8,12,256]{2,0,1:T(8,128)S(1)}, s32[8,12,256]{2,0,1:T(8,128)}, u32[]{:S(2)}) copy-start(s32[8,12,256]{2,0,1:T(8,128)} %param.8) | copy-start | bytes 294916
  3.4 0.8 %copy-start.3 = (bf16[256,128]{1,0:T(8,128)(2,1)S(1)}, bf16[256,128]{1,0:T(8,128)(2,1)}, u32[]{:S(2)}) copy-start(bf16[256,128]{1,0:T(8,128)(2,1)} %q_in.1) | copy-start | bytes 196612
  4.3 0.8 %copy-start.4 = (bf16[256,128]{1,0:T(8,128)(2,1)S(1)}, bf16[256,128]{1,0:T(8,128)(2,1)}, u32[]{:S(2)}) copy-start(bf16[256,128]{1,0:T(8,128)(2,1)} %k_in.1) | copy-start | bytes 196612
where the time goes:
time: 35.2 us; the launch traced here: 34.8 us
  Pallas kernels  27 us (77%)
  local copies, waits for them, and re-layouts  7.1 us (20%)
  between operations  0.65 us (2%)
    pallas_call x1, Pallas kernels, per_device(): pl.pallas_call(functools.partial(kernel, n_seq, n_head), out_shape=(jax.S...  27 us
    unnamed x14, local copies, waits for them, and re-layouts  7.1 us

commit v1 on v0

--- a/solution.py
+++ b/solution.py
@@ -12,6 +12,7 @@
 LANES = 128
 SCALE_CODE = 0.125
 MESH = pl.DeviceIdType.MESH
+PIECES = 8
 
 
 def dot(a, b, da, db):
@@ -21,11 +22,14 @@
 def kernel(
     n_seq, n_head,
     q_in, k_in, v_in, code_in, g_in,
-    att_out, qg_out, kg_out, vg_out,
+    *rest,
+):
+    att_outs, vg_outs = rest[:PIECES], rest[PIECES:2 * PIECES]
+    (
+    qg_out, kg_out,
     att, vg, qg, kg, wts, lams, own, got, pend, back, racc, qk_send, qk_recv,
     f_send, f_recv, b_send, b_recv, h_send, h_recv,
-    q_ref, k_ref, v_ref, code_ref, g_ref, load,
-):
+    q_ref, k_ref, v_ref, code_ref, g_ref, load) = rest[2 * PIECES:]
     loads = [
         pltpu.make_async_copy(src, dst, load.at[i])
         for i, (src, dst) in enumerate((
@@ -343,7 +347,9 @@
         step_forward(low_bits + 2, c)
     consume(top)
     send_share(0, qg[...])
-    att_out[...] = att[...].astype(bf16)
+    part = tokens // PIECES
+    for p in range(PIECES):
+        att_outs[p][...] = att[p * part:(p + 1) * part, :].astype(bf16)
     for stage in range(3, stages):
         for c in range(chunks):
             step_backward(stage, c)
@@ -361,10 +367,10 @@
         incoming = racc[c]
         low = (incoming + near_sum[:, cols[c]]).astype(bf16)
         high = incoming.astype(bf16)
-        vg_out[first_half, cols[c]] = (
-            vg[first_half, cols[c]] + dot(k_ref[first_half, :], low, 1, 0)).astype(bf16)
-        vg_out[second_half, cols[c]] = (
-            vg[second_half, cols[c]] + dot(k_ref[second_half, :], high, 1, 0)).astype(bf16)
+        for half, state in ((first_half, low), (second_half, high)):
+            final = (vg[half, cols[c]] + dot(k_ref[half, :], state, 1, 0)).astype(bf16)
+            for p in range(PIECES // 2):
+                vg_outs[half.start // part + p][:, cols[c]] = final[p * part:(p + 1) * part]
 
     for which, out in ((0, qg_out), (1, kg_out)):
         total = qk_send[which, head]
@@ -416,16 +422,15 @@
     vmem = pl.BlockSpec(memory_space=pltpu.VMEM)
     links = (bits, chunks, depth, LANES)
     dma = pltpu.SemaphoreType.DMA
-    return pl.pallas_call(
+    results = pl.pallas_call(
         functools.partial(kernel, n_seq, n_head),
         out_shape=(
-            jax.ShapeDtypeStruct((tokens, total_width), bf16),
+            *[jax.ShapeDtypeStruct((tokens // PIECES, total_width), bf16)] * (2 * PIECES),
             jax.ShapeDtypeStruct((rows, depth), f32),
             jax.ShapeDtypeStruct((rows, depth), f32),
-            jax.ShapeDtypeStruct((tokens, total_width), bf16),
         ),
         in_specs=[pl.BlockSpec(memory_space=pltpu.HBM)] * 5,
-        out_specs=(vmem,) * 4,
+        out_specs=(vmem,) * (2 * PIECES + 2),
         scratch_shapes=[
             pltpu.VMEM((tokens, total_width), f32),
             pltpu.VMEM((tokens, total_width), f32),
@@ -454,8 +459,38 @@
             dma((5,)),
         ],
         compiler_params=pltpu.CompilerParams(
-            collective_id=0, has_side_effects=True, vmem_limit_bytes=40 * 1024 * 1024),
+            collective_id=0, has_side_effects=True, vmem_limit_bytes=54656 * 1024),
     )(queries, keys, values, jnp.transpose(level_codes, (1, 0, 2)), cotangent)
+    return hand_over(tokens, total_width, results)
+
+
+def settle(*refs):
+    att_parts, vg_parts = refs[:PIECES], refs[PIECES:2 * PIECES]
+    qg, kg, att_out, qg_out, kg_out, vg_out, sems = refs[2 * PIECES:]
+    part = att_parts[0].shape[0]
+    pairs = [(qg, qg_out), (kg, kg_out)]
+    for p in range(PIECES):
+        pairs.append((att_parts[p], att_out.at[pl.ds(p * part, part)]))
+        pairs.append((vg_parts[p], vg_out.at[pl.ds(p * part, part)]))
+    copies = [pltpu.make_async_copy(a, b, sems.at[i]) for i, (a, b) in enumerate(pairs)]
+    for one in copies:
+        one.start()
+    for one in copies:
+        one.wait()
+
+
+def hand_over(tokens, total_width, results):
+    wide = jax.ShapeDtypeStruct((tokens, total_width), jnp.bfloat16)
+    thin = jax.ShapeDtypeStruct(results[-1].shape, jnp.float32)
+    anywhere = pl.BlockSpec(memory_space=pl.ANY)
+    return pl.pallas_call(
+        settle,
+        out_shape=(wide, thin, thin, wide),
+        in_specs=[anywhere] * len(results),
+        out_specs=(anywhere,) * 4,
+        scratch_shapes=[pltpu.SemaphoreType.DMA((len(results),))],
+        compiler_params=pltpu.CompilerParams(vmem_limit_bytes=1024 * 1024),
+    )(*results)
 
 
 def solution(mesh):

time: 35.2 us -> 29.4 us (0.84)
  the two profiles are of different devices: /device:TPU:27 before, /device:TPU:0 now
where the time goes in v1:
time: 29.4 us; the launch traced here: 29.2 us
  Pallas kernels  28.6 us (97%)
  between operations  0.64 us (2%)
    pallas_call x1, Pallas kernels, per_device(): pl.pallas_call(functools.partial(kernel, n_seq, n_head), out_shape=(*[jax...  27.6 us
    pallas_call x1, Pallas kernels, hand_over(): pl.pallas_call(settle, out_shape=(wide, thin, thin, wide), in_specs=[anyw...  0.97 us

profile of v1, /device:TPU:0, one launch (start us, length us, event | category | flops | bytes accessed | tf_op | source)
XLA Modules:
  0.0 29.2 jit_solution(11546758331946771282)
XLA Ops:
  0.6 27.6 %shard_map.84 = (bf16[32,512]{1,0:T(8,128)(2,1)S(1)}, bf16[32,512]{1,0:T(8,128)(2,1)S(1)}, bf16[32,512]{1,0:T(8,128)(2,1)S(1)}, bf16[32,512]{1,0:T(8,128)(2,1)S(...) custom-call(bf16[256,128]{1,0:T(8,128)(2,1)} %q_in.1, ...), custom_call_target="tpu_custom_call" | custom-call | tf_op jit(solution)/shard_map/pallas_call | solution.py:425
  28.3 1.0 %shard_map.85 = (bf16[256,512]{1,0:T(8,128)(2,1)}, f32[64,128]{1,0:T(8,128)}, f32[64,128]{1,0:T(8,128)}, bf16[256,512]{1,0:T(8,128)(2,1)}) custom-call(bf16[32,512]{1,0:T(8,128)(2,1)S(1)} %get-tuple-element.22.refs_0_, bf16[32,512]{1,0:T(8,128)(2,1)S(1)} %get-tuple-element.23.refs_1_, bf16[32,512]{1,0:T(8,128)(2,1)S(1)} %get-tuple-element.24.refs_2_, ...), custom_call_target="tpu_custom_call" | custom-call | tf_op jit(solution)/shard_map/pallas_call | solution.py:486

commit v2 on v1

--- a/solution.py
+++ b/solution.py
@@ -13,6 +13,7 @@
 SCALE_CODE = 0.125
 MESH = pl.DeviceIdType.MESH
 PIECES = 8
+ROOM = 54656 * 1024
 
 
 def dot(a, b, da, db):
@@ -412,7 +413,7 @@
             backward(top, c).wait_send()
 
 
-def per_device(n_seq, n_head, queries, keys, values, level_codes, cotangent):
+def on_any(n_seq, n_head, queries, keys, values, level_codes, cotangent):
     tokens, depth = queries.shape
     total_width = values.shape[1]
     chunks = total_width // LANES
@@ -459,7 +460,7 @@
             dma((5,)),
         ],
         compiler_params=pltpu.CompilerParams(
-            collective_id=0, has_side_effects=True, vmem_limit_bytes=54656 * 1024),
+            collective_id=0, has_side_effects=True, vmem_limit_bytes=ROOM),
     )(queries, keys, values, jnp.transpose(level_codes, (1, 0, 2)), cotangent)
     return hand_over(tokens, total_width, results)
 
@@ -491,6 +492,622 @@
         scratch_shapes=[pltpu.SemaphoreType.DMA((len(results),))],
         compiler_params=pltpu.CompilerParams(vmem_limit_bytes=1024 * 1024),
     )(*results)
+
+
+SUBS = 2
+AHEAD = (3, 2, 1)
+
+
+def line_kernel(n_head, names, q_in, k_in, v_in, code_in, g_in, *rest):
+    att_outs, vg_outs = rest[:PIECES], rest[PIECES:2 * PIECES]
+    qg_out, kg_out = rest[2 * PIECES:2 * PIECES + 2]
+    r = dict(zip(names, rest[2 * PIECES + 2:]))
+    att, vg, qg, kg, wts, lams = (r[n] for n in ("att", "vg", "qg", "kg", "wts", "lams"))
+    own, sx, rr, gm, tt, gt = (r[n] for n in ("own", "sx", "rr", "gm", "tt", "gt"))
+    w0, wmid, wtop, rz, zz, gz = (r[n] for n in ("w0", "wmid", "wtop", "rz", "zz", "gz"))
+    ux, us, gu, g0, hb, hs, hx = (r[n] for n in ("ux", "us", "gu", "g0", "hb", "hs", "hx"))
+    nearby, qk_send, qk_recv = (r[n] for n in ("nearby", "qk_send", "qk_recv"))
+    q_ref, k_ref, v_ref, code_ref, g_ref = (r[n] for n in ("q", "k", "v", "code", "g"))
+    load, entry = r["load"], r["entry"]
+
+    loads = [
+        pltpu.make_async_copy(src, dst, load.at[i])
+        for i, (src, dst) in enumerate((
+            (k_in, k_ref), (v_in, v_ref), (g_in, g_ref), (q_in, q_ref), (code_in, code_ref)))
+    ]
+    for one in loads:
+        one.start()
+    tokens, depth = q_ref.shape
+    total_width = v_ref.shape[1]
+    heads = code_ref.shape[1]
+    width = total_width // heads
+    chunks = total_width // LANES
+    per_chunk = LANES // width
+    blocks = tokens // STRETCH
+    share_rows = tokens // n_head
+    scale = depth ** -0.5
+    near = STRETCH_BITS + 1
+    far = near + 1
+    top, mid = 2, 1
+    half_width = total_width // 2
+    f32, bf16 = jnp.float32, jnp.bfloat16
+    seq, head = lax.axis_index("seq"), lax.axis_index("head")
+    x = lax.rem(seq, 2)
+    line = lax.div(seq, 2)
+    low = lax.rem(line, 2)
+    across = seq + 1 - 2 * x
+    peers = [lax.rem(head + j, n_head) for j in range(1, n_head)]
+
+    def when(*conditions):
+        return pl.when(functools.reduce(jnp.logical_and, conditions))
+
+    left, right = x == 0, x == 1
+    early, late = line < 2, line >= 2
+    even, odd = low == 0, low == 1
+    barrier = pltpu.get_barrier_semaphore()
+
+    def greet(to, sem=barrier):
+        pl.semaphore_signal(sem, inc=1, device_id=to, device_id_type=MESH)
+
+    greet((across, head))
+    for peer in peers:
+        greet((seq, peer))
+
+    @when(line == 0)
+    def _():
+        greet((seq + 2, head))
+
+    @when(early)
+    def _():
+        greet((x + 4, head))
+        greet((x + 6, head))
+
+    @when(late)
+    def _():
+        greet((seq + 2 - 4 * low, head))
+        greet((across + 2 - 4 * low, head))
+
+    def rows(s):
+        return pl.ds(s * (depth // SUBS), depth // SUBS)
+
+    subs = [(j, s) for j in range(2) for s in range(SUBS)]
+
+    def mine(j):
+        return 2 * x + j
+
+    def other(j):
+        return 2 * (1 - x) + j
+
+    def remote(src, dst, send, recv, to):
+        return pltpu.make_async_remote_copy(
+            src_ref=src, dst_ref=dst, send_sem=send, recv_sem=recv,
+            device_id=(to, head), device_id_type=MESH)
+
+    def f1(c, s):
+        return remote(own.at[c, rows(s)], sx.at[c, rows(s)],
+                      r["f1s"].at[c, s], r["f1r"].at[c, s], across)
+
+    def f2(j, s):
+        return remote(rr.at[j, rows(s)], gm.at[mine(j), rows(s)],
+                      r["f2s"].at[j, s], r["f2r"].at[j, s], seq + 2)
+
+    def agm(c, j, s):
+        return remote(gm.at[c, rows(s)], gm.at[c, rows(s)],
+                      r["agms"].at[j, s], r["agmr"].at[j, s], across)
+
+    def f3(d, j, s):
+        return remote(tt.at[j, rows(s)], gt.at[mine(j), rows(s)],
+                      r["f3s"].at[d, j, s], r["f3r"].at[j, s], seq + 4 - 2 * d)
+
+    def agt(c, j, s):
+        return remote(gt.at[c, rows(s)], gt.at[c, rows(s)],
+                      r["agts"].at[j, s], r["agtr"].at[j, s], across)
+
+    def b1(i, s):
+        there_x = x if i % 2 == 0 else 1 - x
+        there_low = low if i < 2 else 1 - low
+        to = seq + (there_x - x) + 2 * (there_low - low)
+        return remote(wtop.at[2 * there_x + there_low, rows(s)], rz.at[i - 1, rows(s)],
+                      r["b1s"].at[i - 1, s], r["b1r"].at[i - 1, s], to)
+
+    def b2(d, j, s):
+        return remote(zz.at[rows(s)], gz.at[j, rows(s)],
+                      r["b2s"].at[d, s], r["b2r"].at[j, s], x + 2 * d)
+
+    def u1(c, j):
+        return remote(wmid.at[c], ux.at[j], r["u1s"].at[j], r["u1r"].at[j], across)
+
+    def u2(j):
+        return remote(us.at[j], gu.at[j], r["u2s"].at[j], r["u2r"].at[j], seq - 2)
+
+    def w0a(j):
+        return remote(w0.at[j], g0.at[j], r["w0s"].at[j], r["w0r"].at[j], across)
+
+    def agb(j, s):
+        return remote(hs.at[j, rows(s)], hx.at[j, rows(s)],
+                      r["agbs"].at[j, s], r["agbr"].at[j, s], across)
+
+    def share(which, j):
+        return pltpu.make_async_remote_copy(
+            src_ref=qk_send.at[which, peers[j]], dst_ref=qk_recv.at[which, j],
+            send_sem=r["hs_"].at[which, j], recv_sem=r["hr_"].at[which, j],
+            device_id=(seq, peers[j]), device_id_type=MESH)
+
+    def send_share(which, grad):
+        for i in range(n_head):
+            qk_send[which, i] = grad[i * share_rows:(i + 1) * share_rows]
+        for j in (1, 2, 0) if n_head == 4 else range(n_head - 1):
+            share(which, j).start()
+
+    cols = [slice(c * LANES, (c + 1) * LANES) for c in range(chunks)]
+    spread = (
+        lax.broadcasted_iota(jnp.int32, (heads, total_width), 1) // width
+        == lax.broadcasted_iota(jnp.int32, (heads, total_width), 0)
+    ).astype(f32)
+
+    def level_weights(level):
+        lam = code_ref[level].astype(f32) * SCALE_CODE
+        return dot(lam, spread, 0, 0)
+
+    def prepare(b, into):
+        lam = level_weights(far + b)
+        lams[b] = lam.astype(bf16)
+        weighted = (g_ref[...].astype(f32) * lam).astype(bf16)
+        wts[b] = weighted
+        sending = dot(q_ref[...], weighted, 0, 0) * scale
+        for c in range(chunks):
+            into[c] = sending[:, cols[c]]
+
+    first_half = slice(0, STRETCH)
+    second_half = slice(STRETCH, 2 * STRETCH)
+    for one in loads:
+        one.wait()
+
+    @when(late)
+    def _():
+        prepare(top, wtop)
+        pl.semaphore_wait(barrier, n_head + 4)
+        for s in range(SUBS):
+            for i in AHEAD:
+                b1(i, s).start()
+        greet((x + 2, head), entry)
+
+    state_low = dot(k_ref[first_half, :], v_ref[first_half, :], 0, 0)
+    state_all = state_low + dot(k_ref[second_half, :], v_ref[second_half, :], 0, 0)
+    for c in range(chunks):
+        own[c] = state_all[:, cols[c]]
+
+    @when(line == 0)
+    def _():
+        pl.semaphore_wait(barrier, n_head)
+
+    @when(line == 1)
+    def _():
+        pl.semaphore_wait(barrier, n_head + 1)
+        greet((x, head), entry)
+
+    @when(line < 3)
+    def _():
+        for j, s in subs:
+            f1(other(j), s).start()
+
+    @when(odd)
+    def _():
+        prepare(mid, wmid)
+        for j in range(2):
+            u1(other(j), j).start()
+
+    @when(right)
+    def _():
+        prepare(0, w0)
+
+    key_pos = lax.rem(lax.broadcasted_iota(jnp.int32, (per_chunk * STRETCH, STRETCH), 0), STRETCH)
+    query_pos = lax.broadcasted_iota(jnp.int32, (per_chunk * STRETCH, STRETCH), 1)
+    differ = jnp.bitwise_xor(query_pos, key_pos)
+    causal = key_pos <= query_pos
+    lane_head = lax.broadcasted_iota(jnp.int32, (STRETCH, LANES), 1) // width
+
+    def split_heads(block):
+        block = block.astype(f32)
+        return jnp.concatenate(
+            [jnp.where(lane_head == i, block, 0.0) for i in range(per_chunk)], axis=0).astype(bf16)
+
+    def do_block(n):
+        at = slice(n * STRETCH, (n + 1) * STRETCH)
+        one = dot(k_ref[at, :], q_ref[at, :], 1, 1) * scale
+        scores = jnp.concatenate([one] * per_chunk, axis=0)
+        press_sum = jnp.zeros((STRETCH, STRETCH), f32)
+        for c in range(chunks):
+            def rows_of(level):
+                parts = []
+                for i in range(per_chunk):
+                    row = code_ref[level, c * per_chunk + i:c * per_chunk + i + 1, at].astype(f32) * SCALE_CODE
+                    parts.append(jnp.broadcast_to(row, (STRETCH, STRETCH)))
+                return jnp.concatenate(parts, axis=0)
+
+            mask = rows_of(STRETCH_BITS)
+            for level in range(STRETCH_BITS - 1, -1, -1):
+                mask = jnp.where(differ < (1 << level), rows_of(level), mask)
+            mask = jnp.where(causal, mask, 0.0)
+            mixed = (scores * mask).astype(bf16)
+            v_split = split_heads(v_ref[at, cols[c]])
+            g_block = g_ref[at, cols[c]]
+            att[at, cols[c]] = dot(mixed, v_split, 0, 0)
+            wide = jnp.concatenate(
+                [mixed[i * STRETCH:(i + 1) * STRETCH] for i in range(per_chunk)], axis=1)
+            vg[at, cols[c]] = dot(wide, split_heads(g_block), 1, 0)
+            press = dot(v_split, g_block, 1, 1) * mask
+            for i in range(per_chunk):
+                press_sum = press_sum + press[i * STRETCH:(i + 1) * STRETCH]
+        press_sum = press_sum.astype(bf16)
+        qg[at, :] = dot(press_sum, k_ref[at, :], 0, 0) * scale
+        kg[at, :] = dot(press_sum, q_ref[at, :], 1, 0) * scale
+
+    def near_level():
+        state = state_low.astype(bf16)
+        lam = level_weights(near)[second_half]
+        att[second_half, :] = att[second_half, :] + lam * (
+            dot(q_ref[second_half, :], state, 1, 0) * scale)
+        weighted = (g_ref[second_half, :].astype(f32) * lam).astype(bf16)
+        qg[second_half, :] = qg[second_half, :] + dot(weighted, state, 1, 1) * scale
+        nearby[...] = dot(q_ref[second_half, :], weighted, 0, 0) * scale
+
+    def span(side):
+        return pl.ds(pl.multiple_of(side * half_width, half_width), half_width)
+
+    def read_state(b, side, ref):
+        at = span(side)
+        state = jnp.concatenate([ref[2 * side], ref[2 * side + 1]], axis=1).astype(bf16)
+        reading = dot(q_ref[...], state, 1, 0) * scale
+        total = att[:, at] + reading * lams[b, :, at].astype(f32)
+        qg[...] = qg[...] + dot(wts[b, :, at], state, 1, 1) * scale
+        return total
+
+    def consume(b, side, ref):
+        att[:, span(side)] = read_state(b, side, ref)
+
+    part = tokens // PIECES
+
+    def write_att(side, total):
+        total = total.astype(bf16)
+        for p in range(PIECES):
+            att_outs[p][:, span(side)] = total[p * part:(p + 1) * part]
+
+    def take_incoming(side, pair):
+        at = span(side)
+        incoming = jnp.concatenate(pair, axis=1)
+        for half, state in (
+                (first_half, incoming + nearby[:, at]), (second_half, incoming)):
+            state = state.astype(bf16)
+            kg[half, :] = kg[half, :] + dot(v_ref[half, at], state, 1, 1)
+            final = (vg[half, at] + dot(k_ref[half, :], state, 1, 0)).astype(bf16)
+            for p in range(PIECES // 2):
+                vg_outs[half.start // part + p][:, at] = final[p * part:(p + 1) * part]
+
+    do_block(0)
+
+    @when(late)
+    def _():
+        for s in range(SUBS):
+            for i in AHEAD:
+                b1(i, s).wait_recv()
+            zz[rows(s)] = (wtop[mine(low), rows(s)] + rz[0, rows(s)]) + (
+                rz[1, rows(s)] + rz[2, rows(s)])
+            b2(0, low, s).start()
+        for s in range(SUBS):
+            b2(1, low, s).start()
+
+    @when(line == 0)
+    def _():
+        pl.semaphore_wait(entry, 1)
+
+    @when(line < 3)
+    def _():
+        for j, s in subs:
+            f1(mine(j), s).wait_recv()
+            rr[j, rows(s)] = own[mine(j), rows(s)] + sx[mine(j), rows(s)]
+
+            @when(even)
+            def _():
+                f2(j, s).start()
+
+    @when(odd)
+    def _():
+        for j in range(2):
+            u1(mine(j), j).wait_recv()
+            us[j] = wmid[mine(j)] + ux[j]
+            u2(j).start()
+
+    @when(left)
+    def _():
+        for j, s in subs:
+            f1(j, s).start()
+
+    @when(left, line == 3)
+    def _():
+        for j, s in subs:
+            f1(2 + j, s).start()
+
+    @when(right)
+    def _():
+        for j in range(2):
+            w0a(j).start()
+
+    do_block(1)
+    near_level()
+
+    @when(line == 1)
+    def _():
+        pl.semaphore_wait(entry, 2)
+        for j, s in subs:
+            f2(j, s).wait_recv()
+            tt[j, rows(s)] = gm[mine(j), rows(s)] + rr[j, rows(s)]
+            f3(0, j, s).start()
+            f3(1, j, s).start()
+        for j, s in subs:
+            agm(mine(j), j, s).start()
+
+    def read_neighbour():
+        @when(right, line < 3)
+        def _():
+            for j, s in subs:
+                f1(j, s).wait_recv()
+
+        @when(right, line == 3)
+        def _():
+            for c in range(chunks):
+                for s in range(SUBS):
+                    f1(c, s).wait_recv()
+
+        @when(right)
+        def _():
+            consume(0, 0, sx)
+            consume(0, 1, sx)
+
+    def read_mid():
+        consume(mid, x, gm)
+        for j, s in subs:
+            agm(other(j), j, s).wait_recv()
+        consume(mid, 1 - x, gm)
+
+    def pass_across(j, s, total):
+        hb[j, rows(s)] = total
+
+        @when(left)
+        def _():
+            hs[j, rows(s)] = total
+
+        @when(right)
+        def _():
+            hs[j, rows(s)] = total + w0[2 + j, rows(s)]
+
+        agb(j, s).start()
+
+    def take_own():
+        @when(left)
+        def _():
+            for j in range(2):
+                w0a(j).wait_recv()
+                hb[j] = hb[j] + g0[j]
+        take_incoming(x, [hb[0], hb[1]])
+
+    def take_other():
+        for j, s in subs:
+            agb(j, s).wait_recv()
+        take_incoming(1 - x, [hx[0], hx[1]])
+
+    @when(early)
+    def _():
+        read_neighbour()
+
+        @when(line == 1)
+        def _():
+            read_mid()
+
+        send_share(0, qg[...])
+        write_att(0, att[:, :half_width])
+        write_att(1, att[:, half_width:])
+
+        @when(line == 0)
+        def _():
+            for j in range(2):
+                u2(j).wait_recv()
+        for j, s in subs:
+            b2(0, j, s).wait_recv()
+
+            @when(line == 0)
+            def _():
+                gz[j, rows(s)] = gz[j, rows(s)] + gu[j, rows(s)]
+            pass_across(j, s, gz[j, rows(s)])
+        take_own()
+        take_other()
+        send_share(1, kg[...])
+
+    @when(late)
+    def _():
+        @when(line == 2)
+        def _():
+            for j in range(2):
+                u2(j).wait_recv()
+                for s in range(SUBS):
+                    pass_across(j, s, gu[j, rows(s)])
+
+        @when(line == 3)
+        def _():
+            for j, s in subs:
+                hb[j, rows(s)] = jnp.zeros((depth // SUBS, LANES), f32)
+
+            @when(right)
+            def _():
+                for j, s in subs:
+                    hs[j, rows(s)] = w0[2 + j, rows(s)]
+                    hx[j, rows(s)] = jnp.zeros((depth // SUBS, LANES), f32)
+                    agb(j, s).start()
+            for j, s in subs:
+                f2(j, s).wait_recv()
+                agm(mine(j), j, s).start()
+
+        for j, s in subs:
+            f3(0, j, s).wait_recv()
+            agt(mine(j), j, s).start()
+        read_neighbour()
+
+        @when(line == 3)
+        def _():
+            read_mid()
+
+        take_own()
+
+        @when(jnp.logical_or(left, line == 2))
+        def _():
+            for j, s in subs:
+                agb(j, s).wait_recv()
+        take_incoming(1 - x, [hx[0], hx[1]])
+        send_share(1, kg[...])
+        write_att(x, read_state(top, x, gt))
+        for j, s in subs:
+            agt(other(j), j, s).wait_recv()
+        total = read_state(top, 1 - x, gt)
+        send_share(0, qg[...])
+        write_att(1 - x, total)
+
+    def collect(which, out):
+        total = qk_send[which, head]
+        for j in range(n_head - 1):
+            share(which, j).wait_recv()
+            total = total + qk_recv[which, j]
+        out[...] = total
+
+    collect(0, qg_out)
+    collect(1, kg_out)
+
+    for which in range(2):
+        for j in range(n_head - 1):
+            share(which, j).wait_send()
+
+    @when(line < 3)
+    def _():
+        for j, s in subs:
+            f1(other(j), s).wait_send()
+
+    @when(left)
+    def _():
+        for j, s in subs:
+            f1(j, s).wait_send()
+
+    @when(left, line == 3)
+    def _():
+        for j, s in subs:
+            f1(2 + j, s).wait_send()
+
+    @when(even)
+    def _():
+        for j, s in subs:
+            f2(j, s).wait_send()
+
+    @when(odd)
+    def _():
+        for j, s in subs:
+            agm(mine(j), j, s).wait_send()
+        for j in range(2):
+            u1(other(j), j).wait_send()
+            u2(j).wait_send()
+
+    @when(line == 1)
+    def _():
+        for j, s in subs:
+            f3(0, j, s).wait_send()
+            f3(1, j, s).wait_send()
+
+    @when(late)
+    def _():
+        for j, s in subs:
+            agt(mine(j), j, s).wait_send()
+        for s in range(SUBS):
+            for i in AHEAD:
+                b1(i, s).wait_send()
+            for d in range(2):
+                b2(d, low, s).wait_send()
+
+    @when(right)
+    def _():
+        for j in range(2):
+            w0a(j).wait_send()
+
+    @when(jnp.logical_or(right, line < 3))
+    def _():
+        for j, s in subs:
+            agb(j, s).wait_send()
+
+
+def line_scratch(tokens, depth, total_width, code_shape, n_head):
+    chunks = total_width // LANES
+    rows = tokens // n_head
+    f32, bf16 = jnp.float32, jnp.bfloat16
+    dma = pltpu.SemaphoreType.DMA
+
+    def states(*lead):
+        return pltpu.VMEM((*lead, depth, LANES), f32)
+
+    return {
+        "att": pltpu.VMEM((tokens, total_width), f32),
+        "vg": pltpu.VMEM((tokens, total_width), f32),
+        "qg": pltpu.VMEM((tokens, depth), f32),
+        "kg": pltpu.VMEM((tokens, depth), f32),
+        "wts": pltpu.VMEM((3, tokens, total_width), bf16),
+        "lams": pltpu.VMEM((3, tokens, total_width), bf16),
+        **{n: states(chunks) for n in ("own", "sx", "gm", "gt", "w0", "wmid", "wtop")},
+        **{n: states(2) for n in ("rr", "tt", "gz", "ux", "us", "gu", "g0", "hb", "hs", "hx")},
+        "rz": states(3),
+        "zz": states(),
+        "nearby": pltpu.VMEM((depth, total_width), f32),
+        "qk_send": pltpu.VMEM((2, n_head, rows, depth), f32),
+        "qk_recv": pltpu.VMEM((2, n_head - 1, rows, depth), f32),
+        "q": pltpu.VMEM((tokens, depth), bf16),
+        "k": pltpu.VMEM((tokens, depth), bf16),
+        "v": pltpu.VMEM((tokens, total_width), bf16),
+        "code": pltpu.VMEM((code_shape[1], code_shape[0], tokens), jnp.int32),
+        "g": pltpu.VMEM((tokens, total_width), bf16),
+        **{n: dma((chunks, SUBS)) for n in ("f1s", "f1r")},
+        **{n: dma((2, SUBS)) for n in (
+            "f2s", "f2r", "agms", "agmr", "f3r", "agts", "agtr", "b2s", "b2r", "agbs", "agbr")},
+        "f3s": dma((2, 2, SUBS)),
+        **{n: dma((3, SUBS)) for n in ("b1s", "b1r")},
+        **{n: dma((2,)) for n in ("u1s", "u1r", "u2s", "u2r", "w0s", "w0r")},
+        **{n: dma((2, n_head - 1)) for n in ("hs_", "hr_")},
+        "load": dma((5,)),
+        "entry": pltpu.SemaphoreType.REGULAR,
+    }
+
+
+def on_line(n_head, queries, keys, values, level_codes, cotangent):
+    tokens, depth = queries.shape
+    total_width = values.shape[1]
+    rows = tokens // n_head
+    f32, bf16 = jnp.float32, jnp.bfloat16
+    vmem = pl.BlockSpec(memory_space=pltpu.VMEM)
+    scratch = line_scratch(tokens, depth, total_width, level_codes.shape, n_head)
+    results = pl.pallas_call(
+        functools.partial(line_kernel, n_head, tuple(scratch)),
+        out_shape=(
+            *[jax.ShapeDtypeStruct((tokens // PIECES, total_width), bf16)] * (2 * PIECES),
+            jax.ShapeDtypeStruct((rows, depth), f32),
+            jax.ShapeDtypeStruct((rows, depth), f32),
+        ),
+        in_specs=[pl.BlockSpec(memory_space=pltpu.HBM)] * 5,
+        out_specs=(vmem,) * (2 * PIECES + 2),
+        scratch_shapes=list(scratch.values()),
+        compiler_params=pltpu.CompilerParams(
+            collective_id=1, has_side_effects=True, vmem_limit_bytes=ROOM),
+    )(queries, keys, values, jnp.transpose(level_codes, (1, 0, 2)), cotangent)
+    return hand_over(tokens, total_width, results)
+
+
+def per_device(n_seq, n_head, queries, keys, values, level_codes, cotangent):
+    suits = n_seq == 8 and n_head == 4 and values.shape[1] == 4 * LANES and queries.shape[0] == 2 * STRETCH
+    if suits:
+        return on_line(n_head, queries, keys, values, level_codes, cotangent)
+    return on_any(n_seq, n_head, queries, keys, values, level_codes, cotangent)
 
 
 def solution(mesh):

time: 29.4 us -> 28.4 us (0.966)
  the two profiles are of different devices: /device:TPU:0 before, /device:TPU:27 now
where the time goes in v2:
time: 28.4 us; the launch traced here: 28.3 us
  Pallas kernels  27.6 us (97%)
  between operations  0.64 us (2%)
    pallas_call x1, Pallas kernels, on_line(): pl.pallas_call(functools.partial(line_kernel, n_head, tuple(scratch)), ou...  26.7 us
    pallas_call x1, Pallas kernels, hand_over(): pl.pallas_call(settle, out_shape=(wide, thin, thin, wide), in_specs=[anyw...  0.97 us

profile of v2, /device:TPU:27, one launch (start us, length us, event | category | flops | bytes accessed | tf_op | source)
XLA Modules:
  0.0 28.3 jit_solution(17011158917053661448)
XLA Ops:
  0.6 26.7 %shard_map.84 = (bf16[32,512]{1,0:T(8,128)(2,1)S(1)}, bf16[32,512]{1,0:T(8,128)(2,1)S(1)}, bf16[32,512]{1,0:T(8,128)(2,1)S(1)}, bf16[32,512]{1,0:T(8,128)(2,1)S(...) custom-call(bf16[256,128]{1,0:T(8,128)(2,1)} %q_in.1, ...), custom_call_target="tpu_custom_call" | custom-call | tf_op jit(solution)/shard_map/pallas_call | solution.py:1090
  27.3 1.0 %shard_map.85 = (bf16[256,512]{1,0:T(8,128)(2,1)}, f32[64,128]{1,0:T(8,128)}, f32[64,128]{1,0:T(8,128)}, bf16[256,512]{1,0:T(8,128)(2,1)}) custom-call(bf16[32,512]{1,0:T(8,128)(2,1)S(1)} %get-tuple-element.22.refs_0_, bf16[32,512]{1,0:T(8,128)(2,1)S(1)} %get-tuple-element.23.refs_1_, bf16[32,512]{1,0:T(8,128)(2,1)S(1)} %get-tuple-element.24.refs_2_, ...), custom_call_target="tpu_custom_call" | custom-call | tf_op jit(solution)/shard_map/pallas_call | solution.py:487

commit v3 on v2

--- a/solution.py
+++ b/solution.py
@@ -505,7 +505,8 @@
     att, vg, qg, kg, wts, lams = (r[n] for n in ("att", "vg", "qg", "kg", "wts", "lams"))
     own, sx, rr, gm, tt, gt = (r[n] for n in ("own", "sx", "rr", "gm", "tt", "gt"))
     w0, wmid, wtop, rz, zz, gz = (r[n] for n in ("w0", "wmid", "wtop", "rz", "zz", "gz"))
-    ux, us, gu, g0, hb, hs, hx = (r[n] for n in ("ux", "us", "gu", "g0", "hb", "hs", "hx"))
+    gu, g0, hb, hs, hx = (r[n] for n in ("gu", "g0", "hb", "hs", "hx"))
+    es = r["es"]
     nearby, qk_send, qk_recv = (r[n] for n in ("nearby", "qk_send", "qk_recv"))
     q_ref, k_ref, v_ref, code_ref, g_ref = (r[n] for n in ("q", "k", "v", "code", "g"))
     load, entry = r["load"], r["entry"]
@@ -536,6 +537,7 @@
     line = lax.div(seq, 2)
     low = lax.rem(line, 2)
     across = seq + 1 - 2 * x
+    first = x + low * (1 - 2 * x)
     peers = [lax.rem(head + j, n_head) for j in range(1, n_head)]
 
     def when(*conditions):
@@ -562,6 +564,10 @@
         greet((x + 4, head))
         greet((x + 6, head))
 
+    @when(line == 1)
+    def _():
+        greet((7 - x, head))
+
     @when(late)
     def _():
         greet((seq + 2 - 4 * low, head))
@@ -587,9 +593,9 @@
         return remote(own.at[c, rows(s)], sx.at[c, rows(s)],
                       r["f1s"].at[c, s], r["f1r"].at[c, s], across)
 
-    def f2(j, s):
-        return remote(rr.at[j, rows(s)], gm.at[mine(j), rows(s)],
-                      r["f2s"].at[j, s], r["f2r"].at[j, s], seq + 2)
+    def f2(c, s):
+        return remote(rr.at[c, rows(s)], gm.at[c, rows(s)],
+                      r["f2s"].at[c, s], r["f2r"].at[c, s], seq + 2)
 
     def agm(c, j, s):
         return remote(gm.at[c, rows(s)], gm.at[c, rows(s)],
@@ -597,11 +603,11 @@
 
     def f3(d, j, s):
         return remote(tt.at[j, rows(s)], gt.at[mine(j), rows(s)],
-                      r["f3s"].at[d, j, s], r["f3r"].at[j, s], seq + 4 - 2 * d)
+                      r["f3s"].at[d, j, s], r["f3r"].at[j, s], seq + 2 if d == 1 else across + 4)
 
     def agt(c, j, s):
         return remote(gt.at[c, rows(s)], gt.at[c, rows(s)],
-                      r["agts"].at[j, s], r["agtr"].at[j, s], across)
+                      r["agts"].at[j, s], r["agtr"].at[j, s], seq + 2 - 4 * low)
 
     def b1(i, s):
         there_x = x if i % 2 == 0 else 1 - x
@@ -614,14 +620,11 @@
         return remote(zz.at[rows(s)], gz.at[j, rows(s)],
                       r["b2s"].at[d, s], r["b2r"].at[j, s], x + 2 * d)
 
-    def u1(c, j):
-        return remote(wmid.at[c], ux.at[j], r["u1s"].at[j], r["u1r"].at[j], across)
-
-    def u2(j):
-        return remote(us.at[j], gu.at[j], r["u2s"].at[j], r["u2r"].at[j], seq - 2)
-
-    def w0a(j):
-        return remote(w0.at[j], g0.at[j], r["w0s"].at[j], r["w0r"].at[j], across)
+    def raw(c):
+        return remote(wmid.at[c], gu.at[c], r["us_"].at[c], r["ur_"].at[c], seq - 2)
+
+    def e1(j):
+        return remote(es.at[j], g0.at[j], r["e1s"].at[j], r["e1r"].at[j], across)
 
     def agb(j, s):
         return remote(hs.at[j, rows(s)], hx.at[j, rows(s)],
@@ -666,11 +669,18 @@
     @when(late)
     def _():
         prepare(top, wtop)
-        pl.semaphore_wait(barrier, n_head + 4)
+
+        @when(line == 2)
+        def _():
+            pl.semaphore_wait(barrier, n_head + 4)
+
+        @when(line == 3)
+        def _():
+            pl.semaphore_wait(barrier, n_head + 5)
         for s in range(SUBS):
             for i in AHEAD:
                 b1(i, s).start()
-        greet((x + 2, head), entry)
+        greet((first + 2, head), entry)
 
     state_low = dot(k_ref[first_half, :], v_ref[first_half, :], 0, 0)
     state_all = state_low + dot(k_ref[second_half, :], v_ref[second_half, :], 0, 0)
@@ -686,20 +696,34 @@
         pl.semaphore_wait(barrier, n_head + 1)
         greet((x, head), entry)
 
-    @when(line < 3)
+    @when(early)
     def _():
         for j, s in subs:
             f1(other(j), s).start()
 
+    @when(early, jnp.logical_or(line == 0, left))
+    def _():
+        for j, s in subs:
+            f1(mine(j), s).start()
+
     @when(odd)
     def _():
         prepare(mid, wmid)
-        for j in range(2):
-            u1(other(j), j).start()
+
+    @when(line == 1)
+    def _():
+        for half in (other, mine):
+            for j in range(2):
+                raw(half(j)).start()
 
     @when(right)
     def _():
         prepare(0, w0)
+
+        @when(odd)
+        def _():
+            for j in range(2):
+                es[j] = w0[j]
 
     key_pos = lax.rem(lax.broadcasted_iota(jnp.int32, (per_chunk * STRETCH, STRETCH), 0), STRETCH)
     query_pos = lax.broadcasted_iota(jnp.int32, (per_chunk * STRETCH, STRETCH), 1)
@@ -786,6 +810,32 @@
 
     do_block(0)
 
+    @when(line == 2)
+    def _():
+        for j, s in subs:
+            f1(other(j), s).start()
+
+    @when(left, line == 2)
+    def _():
+        for j, s in subs:
+            f1(mine(j), s).start()
+
+    @when(left, line == 3)
+    def _():
+        for half in (0, 2):
+            for j, s in subs:
+                f1(half + j, s).start()
+
+    @when(line == 3)
+    def _():
+        for j in range(2):
+            raw(other(j)).start()
+
+    @when(right, line == 3)
+    def _():
+        for j in range(2):
+            e1(j).start()
+
     @when(late)
     def _():
         for s in range(SUBS):
@@ -801,37 +851,35 @@
     def _():
         pl.semaphore_wait(entry, 1)
 
-    @when(line < 3)
-    def _():
-        for j, s in subs:
-            f1(mine(j), s).wait_recv()
-            rr[j, rows(s)] = own[mine(j), rows(s)] + sx[mine(j), rows(s)]
-
-            @when(even)
-            def _():
-                f2(j, s).start()
-
-    @when(odd)
+    def add_near(j, s):
+        f1(mine(j), s).wait_recv()
+        rr[mine(j), rows(s)] = own[mine(j), rows(s)] + sx[mine(j), rows(s)]
+
+    @when(early)
+    def _():
+        for j, s in subs:
+            add_near(j, s)
+
+            @when(line == 0)
+            def _():
+                f2(mine(j), s).start()
+
+    @when(line == 3)
     def _():
         for j in range(2):
-            u1(mine(j), j).wait_recv()
-            us[j] = wmid[mine(j)] + ux[j]
-            u2(j).start()
-
-    @when(left)
-    def _():
-        for j, s in subs:
-            f1(j, s).start()
-
-    @when(left, line == 3)
-    def _():
-        for j, s in subs:
-            f1(2 + j, s).start()
-
-    @when(right)
+            raw(mine(j)).start()
+
+        @when(right)
+        def _():
+            for j, s in subs:
+                hs[j, rows(s)] = w0[2 + j, rows(s)]
+                hx[j, rows(s)] = jnp.zeros((depth // SUBS, LANES), f32)
+                agb(j, s).start()
+
+    @when(right, line == 1)
     def _():
         for j in range(2):
-            w0a(j).start()
+            e1(j).start()
 
     do_block(1)
     near_level()
@@ -840,15 +888,48 @@
     def _():
         pl.semaphore_wait(entry, 2)
         for j, s in subs:
-            f2(j, s).wait_recv()
-            tt[j, rows(s)] = gm[mine(j), rows(s)] + rr[j, rows(s)]
+            f2(mine(j), s).wait_recv()
+            tt[j, rows(s)] = gm[mine(j), rows(s)] + rr[mine(j), rows(s)]
+            f3(1, j, s).start()
+        for j, s in subs:
             f3(0, j, s).start()
-            f3(1, j, s).start()
-        for j, s in subs:
-            agm(mine(j), j, s).start()
+
+    def pass_raw():
+        for j in range(2):
+            raw(other(j)).wait_recv()
+
+            @when(left)
+            def _():
+                es[j] = gu[2 + j]
+
+            @when(right)
+            def _():
+                es[j] = gu[j] + w0[j]
+            e1(j).start()
+
+    @when(line == 0)
+    def _():
+        pass_raw()
+
+    @when(line == 2)
+    def _():
+        for j, s in subs:
+            add_near(j, s)
+            f2(mine(j), s).start()
+
+    @when(line == 0)
+    def _():
+        for j, s in subs:
+            f1(other(j), s).wait_recv()
+            rr[other(j), rows(s)] = own[other(j), rows(s)] + sx[other(j), rows(s)]
+            f2(other(j), s).start()
+
+    @when(line == 2)
+    def _():
+        pass_raw()
 
     def read_neighbour():
-        @when(right, line < 3)
+        @when(right, jnp.logical_or(line == 1, line == 2))
         def _():
             for j, s in subs:
                 f1(j, s).wait_recv()
@@ -865,10 +946,17 @@
             consume(0, 1, sx)
 
     def read_mid():
-        consume(mid, x, gm)
-        for j, s in subs:
-            agm(other(j), j, s).wait_recv()
-        consume(mid, 1 - x, gm)
+        @when(line == 1)
+        def _():
+            for j, s in subs:
+                f2(other(j), s).wait_recv()
+
+        @when(line == 3)
+        def _():
+            for j, s in subs:
+                agm(other(j), j, s).wait_recv()
+        consume(mid, 0, gm)
+        consume(mid, 1, gm)
 
     def pass_across(j, s, total):
         hb[j, rows(s)] = total
@@ -884,16 +972,21 @@
         agb(j, s).start()
 
     def take_own():
-        @when(left)
+        @when(jnp.logical_or(left, even))
         def _():
             for j in range(2):
-                w0a(j).wait_recv()
+                e1(j).wait_recv()
                 hb[j] = hb[j] + g0[j]
         take_incoming(x, [hb[0], hb[1]])
 
     def take_other():
         for j, s in subs:
             agb(j, s).wait_recv()
+
+        @when(even)
+        def _():
+            for j in range(2):
+                hx[j] = hx[j] + gu[other(j)]
         take_incoming(1 - x, [hx[0], hx[1]])
 
     @when(early)
@@ -911,13 +1004,13 @@
         @when(line == 0)
         def _():
             for j in range(2):
-                u2(j).wait_recv()
+                raw(mine(j)).wait_recv()
         for j, s in subs:
             b2(0, j, s).wait_recv()
 
             @when(line == 0)
             def _():
-                gz[j, rows(s)] = gz[j, rows(s)] + gu[j, rows(s)]
+                gz[j, rows(s)] = gz[j, rows(s)] + gu[mine(j), rows(s)]
             pass_across(j, s, gz[j, rows(s)])
         take_own()
         take_other()
@@ -925,51 +1018,54 @@
 
     @when(late)
     def _():
-        @when(line == 2)
-        def _():
-            for j in range(2):
-                u2(j).wait_recv()
-                for s in range(SUBS):
-                    pass_across(j, s, gu[j, rows(s)])
-
         @when(line == 3)
         def _():
             for j, s in subs:
                 hb[j, rows(s)] = jnp.zeros((depth // SUBS, LANES), f32)
-
-            @when(right)
+            for j, s in subs:
+                f2(mine(j), s).wait_recv()
+                agm(mine(j), j, s).start()
+
+        @when(line == 2)
+        def _():
+            for j in range(2):
+                raw(mine(j)).wait_recv()
+                for s in range(SUBS):
+                    pass_across(j, s, gu[mine(j), rows(s)])
+
+        for j, s in subs:
+            f3(0, j, s).wait_recv()
+            agt(2 * first + j, j, s).start()
+
+        read_neighbour()
+
+        @when(line == 3)
+        def _():
+            read_mid()
+            take_own()
+
+            @when(left)
             def _():
                 for j, s in subs:
-                    hs[j, rows(s)] = w0[2 + j, rows(s)]
-                    hx[j, rows(s)] = jnp.zeros((depth // SUBS, LANES), f32)
-                    agb(j, s).start()
-            for j, s in subs:
-                f2(j, s).wait_recv()
-                agm(mine(j), j, s).start()
-
-        for j, s in subs:
-            f3(0, j, s).wait_recv()
-            agt(mine(j), j, s).start()
-        read_neighbour()
-
-        @when(line == 3)
-        def _():
-            read_mid()
-
-        take_own()
-
-        @when(jnp.logical_or(left, line == 2))
-        def _():
-            for j, s in subs:
-                agb(j, s).wait_recv()
-        take_incoming(1 - x, [hx[0], hx[1]])
-        send_share(1, kg[...])
-        write_att(x, read_state(top, x, gt))
-        for j, s in subs:
-            agt(other(j), j, s).wait_recv()
-        total = read_state(top, 1 - x, gt)
+                    agb(j, s).wait_recv()
+            take_incoming(1 - x, [hx[0], hx[1]])
+            send_share(1, kg[...])
+
+        write_att(first, read_state(top, first, gt))
+
+        @when(line == 2)
+        def _():
+            take_own()
+        for j, s in subs:
+            agt(2 * (1 - first) + j, j, s).wait_recv()
+        total = read_state(top, 1 - first, gt)
         send_share(0, qg[...])
-        write_att(1 - x, total)
+        write_att(1 - first, total)
+
+        @when(line == 2)
+        def _():
+            take_other()
+            send_share(1, kg[...])
 
     def collect(which, out):
         total = qk_send[which, head]
@@ -990,28 +1086,36 @@
         for j, s in subs:
             f1(other(j), s).wait_send()
 
-    @when(left)
-    def _():
-        for j, s in subs:
-            f1(j, s).wait_send()
+    @when(jnp.logical_or(line == 0, jnp.logical_and(line < 3, left)))
+    def _():
+        for j, s in subs:
+            f1(mine(j), s).wait_send()
 
     @when(left, line == 3)
     def _():
-        for j, s in subs:
-            f1(2 + j, s).wait_send()
+        for c in range(chunks):
+            for s in range(SUBS):
+                f1(c, s).wait_send()
 
     @when(even)
     def _():
         for j, s in subs:
-            f2(j, s).wait_send()
+            f2(mine(j), s).wait_send()
+
+    @when(line == 0)
+    def _():
+        for j, s in subs:
+            f2(other(j), s).wait_send()
+
+    @when(line == 3)
+    def _():
+        for j, s in subs:
+            agm(mine(j), j, s).wait_send()
 
     @when(odd)
     def _():
-        for j, s in subs:
-            agm(mine(j), j, s).wait_send()
-        for j in range(2):
-            u1(other(j), j).wait_send()
-            u2(j).wait_send()
+        for c in range(chunks):
+            raw(c).wait_send()
 
     @when(line == 1)
     def _():
@@ -1022,17 +1126,17 @@
     @when(late)
     def _():
         for j, s in subs:
-            agt(mine(j), j, s).wait_send()
+            agt(2 * first + j, j, s).wait_send()
         for s in range(SUBS):
             for i in AHEAD:
                 b1(i, s).wait_send()
             for d in range(2):
                 b2(d, low, s).wait_send()
 
-    @when(right)
+    @when(jnp.logical_or(right, even))
     def _():
         for j in range(2):
-            w0a(j).wait_send()
+            e1(j).wait_send()
 
     @when(jnp.logical_or(right, line < 3))
     def _():
@@ -1056,8 +1160,8 @@
         "kg": pltpu.VMEM((tokens, depth), f32),
         "wts": pltpu.VMEM((3, tokens, total_width), bf16),
         "lams": pltpu.VMEM((3, tokens, total_width), bf16),
-        **{n: states(chunks) for n in ("own", "sx", "gm", "gt", "w0", "wmid", "wtop")},
-        **{n: states(2) for n in ("rr", "tt", "gz", "ux", "us", "gu", "g0", "hb", "hs", "hx")},
+        **{n: states(chunks) for n in ("own", "sx", "gm", "gt", "w0", "wmid", "wtop", "rr", "gu")},
+        **{n: states(2) for n in ("tt", "gz", "es", "g0", "hb", "hs", "hx")},
         "rz": states(3),
         "zz": states(),
         "nearby": pltpu.VMEM((depth, total_width), f32),
@@ -1068,12 +1172,13 @@
         "v": pltpu.VMEM((tokens, total_width), bf16),
         "code": pltpu.VMEM((code_shape[1], code_shape[0], tokens), jnp.int32),
         "g": pltpu.VMEM((tokens, total_width), bf16),
-        **{n: dma((chunks, SUBS)) for n in ("f1s", "f1r")},
+        **{n: dma((chunks, SUBS)) for n in ("f1s", "f1r", "f2s", "f2r")},
         **{n: dma((2, SUBS)) for n in (
-            "f2s", "f2r", "agms", "agmr", "f3r", "agts", "agtr", "b2s", "b2r", "agbs", "agbr")},
+            "agms", "agmr", "f3r", "agts", "agtr", "b2s", "b2r", "agbs", "agbr")},
         "f3s": dma((2, 2, SUBS)),
         **{n: dma((3, SUBS)) for n in ("b1s", "b1r")},
-        **{n: dma((2,)) for n in ("u1s", "u1r", "u2s", "u2r", "w0s", "w0r")},
+        **{n: dma((2,)) for n in ("e1s", "e1r")},
+        **{n: dma((chunks,)) for n in ("us_", "ur_")},
         **{n: dma((2, n_head - 1)) for n in ("hs_", "hr_")},
         "load": dma((5,)),
         "entry": pltpu.SemaphoreType.REGULAR,

time: 28.4 us -> 26.7 us (0.940)
  the two profiles are of different devices: /device:TPU:27 before, /device:TPU:17 now
where the time goes in v3:
time: 26.7 us; the launch traced here: 26.5 us
  Pallas kernels  25.9 us (97%)
  between operations  0.64 us (2%)
    pallas_call x1, Pallas kernels, on_line(): pl.pallas_call(functools.partial(line_kernel, n_head, tuple(scratch)), ou...  24.9 us
    pallas_call x1, Pallas kernels, hand_over(): pl.pallas_call(settle, out_shape=(wide, thin, thin, wide), in_specs=[anyw...  0.97 us

profile of v3, /device:TPU:17, one launch (start us, length us, event | category | flops | bytes accessed | tf_op | source)
XLA Modules:
  0.0 26.5 jit_solution(11376251718033881601)
XLA Ops:
  0.6 24.9 %shard_map.84 = (bf16[32,512]{1,0:T(8,128)(2,1)S(1)}, bf16[32,512]{1,0:T(8,128)(2,1)S(1)}, bf16[32,512]{1,0:T(8,128)(2,1)S(1)}, bf16[32,512]{1,0:T(8,128)(2,1)S(...) custom-call(bf16[256,128]{1,0:T(8,128)(2,1)} %q_in.1, ...), custom_call_target="tpu_custom_call" | custom-call | tf_op jit(solution)/shard_map/pallas_call | solution.py:1195
  25.6 1.0 %shard_map.85 = (bf16[256,512]{1,0:T(8,128)(2,1)}, f32[64,128]{1,0:T(8,128)}, f32[64,128]{1,0:T(8,128)}, bf16[256,512]{1,0:T(8,128)(2,1)}) custom-call(bf16[32,512]{1,0:T(8,128)(2,1)S(1)} %get-tuple-element.22.refs_0_, bf16[32,512]{1,0:T(8,128)(2,1)S(1)} %get-tuple-element.23.refs_1_, bf16[32,512]{1,0:T(8,128)(2,1)S(1)} %get-tuple-element.24.refs_2_, ...), custom_call_target="tpu_custom_call" | custom-call | tf_op jit(solution)/shard_map/pallas_call | solution.py:487

commit v4 on v3

--- a/solution.py
+++ b/solution.py
@@ -890,9 +890,8 @@
         for j, s in subs:
             f2(mine(j), s).wait_recv()
             tt[j, rows(s)] = gm[mine(j), rows(s)] + rr[mine(j), rows(s)]
+            f3(0, j, s).start()
             f3(1, j, s).start()
-        for j, s in subs:
-            f3(0, j, s).start()
 
     def pass_raw():
         for j in range(2):

time: 26.7 us -> 26.2 us (0.981)
  the two profiles are of different devices: /device:TPU:17 before, /device:TPU:27 now
where the time goes in v4:
time: 26.2 us; the launch traced here: 25.7 us
  Pallas kernels  25.1 us (96%)
  between operations  0.64 us (2%)
    pallas_call x1, Pallas kernels, on_line(): pl.pallas_call(functools.partial(line_kernel, n_head, tuple(scratch)), ou...  24.1 us
    pallas_call x1, Pallas kernels, hand_over(): pl.pallas_call(settle, out_shape=(wide, thin, thin, wide), in_specs=[anyw...  0.97 us

profile of v4, /device:TPU:27, one launch (start us, length us, event | category | flops | bytes accessed | tf_op | source)
XLA Modules:
  0.0 25.7 jit_solution(16374990809678141345)
XLA Ops:
  0.6 24.1 %shard_map.84 = (bf16[32,512]{1,0:T(8,128)(2,1)S(1)}, bf16[32,512]{1,0:T(8,128)(2,1)S(1)}, bf16[32,512]{1,0:T(8,128)(2,1)S(1)}, bf16[32,512]{1,0:T(8,128)(2,1)S(...) custom-call(bf16[256,128]{1,0:T(8,128)(2,1)} %q_in.1, ...), custom_call_target="tpu_custom_call" | custom-call | tf_op jit(solution)/shard_map/pallas_call | solution.py:1194
  24.8 1.0 %shard_map.85 = (bf16[256,512]{1,0:T(8,128)(2,1)}, f32[64,128]{1,0:T(8,128)}, f32[64,128]{1,0:T(8,128)}, bf16[256,512]{1,0:T(8,128)(2,1)}) custom-call(bf16[32,512]{1,0:T(8,128)(2,1)S(1)} %get-tuple-element.22.refs_0_, bf16[32,512]{1,0:T(8,128)(2,1)S(1)} %get-tuple-element.23.refs_1_, bf16[32,512]{1,0:T(8,128)(2,1)S(1)} %get-tuple-element.24.refs_2_, ...), custom_call_target="tpu_custom_call" | custom-call | tf_op jit(solution)/shard_map/pallas_call | solution.py:487

commit v5 on v4

--- a/solution.py
+++ b/solution.py
@@ -1021,9 +1021,6 @@
         def _():
             for j, s in subs:
                 hb[j, rows(s)] = jnp.zeros((depth // SUBS, LANES), f32)
-            for j, s in subs:
-                f2(mine(j), s).wait_recv()
-                agm(mine(j), j, s).start()
 
         @when(line == 2)
         def _():
@@ -1036,11 +1033,11 @@
             f3(0, j, s).wait_recv()
             agt(2 * first + j, j, s).start()
 
-        read_neighbour()
-
         @when(line == 3)
         def _():
-            read_mid()
+            for j, s in subs:
+                f2(mine(j), s).wait_recv()
+                agm(mine(j), j, s).start()
             take_own()
 
             @when(left)
@@ -1049,6 +1046,12 @@
                     agb(j, s).wait_recv()
             take_incoming(1 - x, [hx[0], hx[1]])
             send_share(1, kg[...])
+
+        read_neighbour()
+
+        @when(line == 3)
+        def _():
+            read_mid()
 
         write_att(first, read_state(top, first, gt))
 

time: 26.2 us -> 26.3 us (level)
  no operation moved by 1% of the time
where the time goes in v5:
time: 26.3 us; the launch traced here: 25.7 us
  Pallas kernels  25.1 us (95%)
  between operations  0.64 us (2%)
    pallas_call x1, Pallas kernels, on_line(): pl.pallas_call(functools.partial(line_kernel, n_head, tuple(scratch)), ou...  24.1 us
    pallas_call x1, Pallas kernels, hand_over(): pl.pallas_call(settle, out_shape=(wide, thin, thin, wide), in_specs=[anyw...  0.97 us

profile of v5, /device:TPU:27, one launch (start us, length us, event | category | flops | bytes accessed | tf_op | source)
XLA Modules:
  0.0 25.7 jit_solution(15317992372230338362)
XLA Ops:
  0.6 24.1 %shard_map.84 = (bf16[32,512]{1,0:T(8,128)(2,1)S(1)}, bf16[32,512]{1,0:T(8,128)(2,1)S(1)}, bf16[32,512]{1,0:T(8,128)(2,1)S(1)}, bf16[32,512]{1,0:T(8,128)(2,1)S(...) custom-call(bf16[256,128]{1,0:T(8,128)(2,1)} %q_in.1, ...), custom_call_target="tpu_custom_call" | custom-call | tf_op jit(solution)/shard_map/pallas_call | solution.py:1197
  24.8 1.0 %shard_map.85 = (bf16[256,512]{1,0:T(8,128)(2,1)}, f32[64,128]{1,0:T(8,128)}, f32[64,128]{1,0:T(8,128)}, bf16[256,512]{1,0:T(8,128)(2,1)}) custom-call(bf16[32,512]{1,0:T(8,128)(2,1)S(1)} %get-tuple-element.22.refs_0_, bf16[32,512]{1,0:T(8,128)(2,1)S(1)} %get-tuple-element.23.refs_1_, bf16[32,512]{1,0:T(8,128)(2,1)S(1)} %get-tuple-element.24.refs_2_, ...), custom_call_target="tpu_custom_call" | custom-call | tf_op jit(solution)/shard_map/pallas_call | solution.py:487
